TPU v7x, 128 devices: a whole 4x4x4 slice. The times are simulated.
128 devices in a mesh: seq: 8 (over y_lo, z), chan: 16 (over x, y_hi, core).
Axes of the slice: x: 4, y: 4 (y_hi: 2, y_lo: 2; y = y_hi * 2 + y_lo), z: 4, core: 2. Of those that a mesh axis runs over, the one named last changes fastest.
Arguments:
- hidden: bfloat16 [8192, 8192], P('seq', 'chan'), may hold values from -6 to 6
- in_weights: bfloat16 [8192, 24576], P(('seq', 'chan')), may hold values from -0.0625 to 0.0625
- filter_bank: float32 [7, 512], replicated, may hold values from -3 to 3
- assignment: int32 [512], P('chan'), may hold values from 0 to 511, each once
Outputs:
- hyena_out: bfloat16 [8192, 8192], P('seq', 'chan')
Inputs may be any that keep to these rules, and one draw needn't show every extreme that they name: `assignment`: a permutation: every filter is used by exactly one group.
All inputs are finite; a program needn't handle non-finite values.
Results may differ from a plain program's by a relative error of at most 0.001.
Values may be sent and summed in bfloat16 or wider, within the bound.
A program may use at most 128 MiB of HBM per device.

v0:
```python
import jax
import jax.numpy as jnp
from jax import lax
from jax.sharding import PartitionSpec as P

D = 8192
GROUP = 16
TAPS = 7
FILTERS = 512


def shifted(block, axis, distance):
    devices = range(lax.axis_size(axis))
    route = [(i - distance, i) for i in devices if i - distance in devices]
    return lax.ppermute(block, axis, route)


def on_device(hidden, in_weights, filter_bank, assignment):
    chan_count = lax.axis_size("chan")
    local_rows = in_weights.shape[0]
    token_count = hidden.shape[0]
    channels = D // chan_count
    rim_rows = TAPS - 1
    widened = lax.all_gather(hidden, "chan", axis=1, tiled=True)
    total_rows = widened.shape[0]
    sectioned = in_weights.reshape(local_rows, 3, chan_count, channels)
    regrouped = lax.all_to_all(sectioned, "chan", split_axis=2, concat_axis=0, tiled=True)
    regrouped = regrouped.reshape(regrouped.shape[0], 3 * channels)
    projected = jnp.dot(
        widened,
        lax.all_gather(regrouped, "seq", axis=0, tiled=True),
        preferred_element_type=jnp.float32,
    )
    projected = projected.reshape(total_rows, 3, channels)
    query_part = projected[:, 0]
    product = projected[:, 1] * projected[:, 2]
    earlier_products = shifted(product[token_count - rim_rows :], "seq", 1)
    extended = jnp.concatenate([earlier_products, product], axis=0)
    selector = (assignment[:, None] == jnp.arange(FILTERS, dtype=jnp.int32)[None, :]).astype(
        jnp.float32
    )
    picked = jnp.dot(selector, filter_bank.T, precision=lax.Precision.HIGHEST)
    filter_taps = jnp.repeat(picked.T, GROUP, axis=1)
    filtered = jnp.zeros((token_count, channels), jnp.float32)
    for lag_index in range(TAPS):
        begin = rim_rows - lag_index
        filtered = (
            filtered + filter_taps[lag_index][None, :] * extended[begin : begin + token_count]
        )
    return (query_part * filtered).astype(jnp.bfloat16)


def solution(mesh):
    in_specs = (P("seq", "chan"), P(("seq", "chan"), None), P(), P("chan"))
    out_specs = P("seq", "chan")
    return jax.shard_map(
        on_device, mesh=mesh, in_specs=in_specs, out_specs=out_specs, check_vma=False
    )
```

profile of v0, /device:TPU:1, one launch (start us, length us, event | category | flops | bytes accessed | tf_op | source)
XLA Modules:
  0.0 465.4 jit_solution(8645560099047800943)
XLA Ops:
  6.5 0.7 all-gather.3.cloned.1.call-update
  7.3 3.1 copy.19
  10.4 1.8 copy.14
  12.1 59.4 %all_to_all.15 = bf16[64,3,16,512]{3,0,1,2:T(8,128)(2,1)S(1)} all-to-all(bf16[64,3,16,512]{3,0,1,2:T(8,128)(2,1)S(1)} %copy.14), channel_id=1, replica_groups=mesh['seq'=8,'chan'=16] {'chan'}, dimensions={2} | all-to-all | bytes 6291456 | tf_op jit(solution)/shard_map/all_to_all | solution.py:27
  71.5 2.7 copy.15
  74.3 2.7 copy.20
  77.0 0.6 copy-done.2
  77.6 0.2 convolution_bitcast_fusion
  77.8 0.1 broadcast_in_dim.43
  77.9 0.1 broadcast_in_dim.44
  78.1 0.1 broadcast_in_dim.42
  78.2 0.1 broadcast_in_dim.40
  78.4 0.1 broadcast_in_dim.38
  78.5 0.1 broadcast_in_dim.36
  78.9 84.8 %all-gather.3.cloned.1.call-done = bf16[1024,8192]{1,0:T(8,128)(2,1)} async-done(((bf16[1024,512]{1,0:T(8,128)(2,1)}), bf16[1024,8192]{1,0:T(8,128)(2,1)}) %all-gather.3.cloned.1.call-update) | async-done | bytes 16777232 | tf_op jit(solution)/shard_map/all_gather | solution.py:24
  163.7 248.8 %all-gather.5.cloned.1.call-done = bf16[8192,1536]{1,0:T(8,128)(2,1)} async-done(((bf16[1024,1536]{1,0:T(8,128)(2,1)}), bf16[8192,1536]{1,0:T(8,128)(2,1)}) %all-gather.5.cloned.1.call-update) | async-done | bytes 25165840 | tf_op jit(solution)/shard_map/all_gather | solution.py:31
  412.5 32.6 %fusion.20 = f32[1024,1536]{0,1:T(8,128)S(1)} fusion(bf16[1024,8192]{1,0:T(8,128)(2,1)} %all-gather.3.cloned.1.call-done, bf16[8192,1536]{1,0:T(8,128)(2,1)} %all-gather.5.cloned.1.call-done), kind=kOutput, calls=%fused_computation.43 | convolution fusion | flops 25769803776 | bytes 48234496 | tf_op jit(solution)/shard_map/dot_general | solution.py:29
  445.1 0.6 slice_multiply_fusion
  445.7 0.1 slice_bitcast_fusion.1
  445.9 1.3 collective-permute-start
  447.2 0.6 fusion.24
  447.7 4.7 %collective-permute-done = f32[6,512]{0,1:T(8,128)S(1)} collective-permute-done((f32[6,512]{0,1:T(8,128)S(1)}, f32[6,512]{0,1:T(8,128)S(1)}, u32[]{:S(2)}, u32[]{:S(2)}) %collective-permute-start) | collective-permute-done | bytes 12320 | tf_op jit(solution)/shard_map/ppermute | solution.py:15
  452.4 4.8 %fusion.5 = bf16[1024,512]{0,1:T(8,128)(2,1)S(1)} fusion(f32[1024,512]{0,1:T(8,128)S(1)} %fusion.24, f32[6,512]{0,1:T(8,128)S(1)} %collective-permute-done, f32[1024,3,512]{0,2,1:T(8,128)S(1)} %bitcast.40, f32[512]{0:T(512)S(1)} %broadcast_in_dim.44, f32[512]{0:T(512)S(1)} %broadcast_in_dim.42, f32[512]{0:T(512)S(1)} %broadcast_in_dim.40, ...), kind=kLoop, calls=%fused_computation.15 | loop fusion | flops 11010048 | bytes 5269504 | tf_op jit(solution)/shard_map/convert_element_type | solution.py:50
  457.2 1.3 copy.17
  (17 shorter events, 0.7 us)
Async XLA Ops:
  6.5 70.5 %copy-start = (f32[7,512]{1,0:T(8,128)S(1)}, f32[7,512]{1,0:T(8,128)}, u32[]{:S(2)}) copy-start(f32[7,512]{1,0:T(8,128)} %param.6) | copy-start | bytes 43012
  6.5 157.2 %all-gather.3.cloned.1.call-start = ((), (), s32[]{:S(2)}) async-start(), calls=%async_computation.1 | async-start | bytes 17825792 | tf_op jit(solution)/shard_map/all_gather | solution.py:24
  7.3 405.2 %all-gather.5.cloned.1.call-start = ((), (), s32[]{:S(2)}) async-start(), calls=%async_computation.2 | async-start | bytes 28311552 | tf_op jit(solution)/shard_map/all_gather | solution.py:31
  77.0 0.7 copy-start.2
  445.9 6.6 %collective-permute-start = (f32[6,512]{0,1:T(8,128)S(1)}, f32[6,512]{0,1:T(8,128)S(1)}, u32[]{:S(2)}, u32[]{:S(2)}) collective-permute-start(f32[6,512]{0,1:T(8,128)S(1)} %slice_bitcast_fusion.1), channel_id=1, source_target_pairs={{0,16},{16,32},{32,48},{48,64},{64,80},{80,96},{96,112},{1,17},{17... | collective-permute-start | bytes 36872 | tf_op jit(solution)/shard_map/ppermute | solution.py:15
  452.4 6.1 %copy-start.1 = (f32[7,512]{1,0:T(8,128)S(1)}, f32[7,512]{1,0:T(8,128)}, u32[]{:S(2)}) copy-start(f32[7,512]{1,0:T(8,128)} %param.6) | copy-start | bytes 43012
Sparse Core Ops, SparseCore 0:
  9.6 154.0 all-gather.2
  165.4 247.0 all-gather.4
where the time goes:
time: 469 us; the launch traced here: 465 us
  waiting for transfers between devices  339 us (72%)
  blocking collectives  59.4 us (13%)
  matrix products  32.8 us (7%)
  between operations  13.5 us (3%)
  local copies, waits for them, and re-layouts  13.4 us (3%)
  other arithmetic  5.87 us (1%)
    all_gather x1, waiting for transfers between devices, on_device(): lax.all_gather(regrouped, 'seq', axis=0, tiled=True)  249 us
    all_gather x1, waiting for transfers between devices, on_device(): widened = lax.all_gather(hidden, 'chan', axis=1, tiled=True)  84.8 us
    all_to_all x1, blocking collectives, on_device(): lax.all_to_all(sectioned, 'chan', split_axis=2, concat_axis=0, tiled=True)  59.4 us
    dot_general x1, matrix products, on_device(): jnp.dot(widened, lax.all_gather(regrouped, 'seq', axis=0, tiled=True), pr...  32.6 us
  transfers between devices with their start and end apart: 3, of which 3 were waited for; matrix products, arithmetic and copies ran while one was open for 3% of the time, Pallas kernels for 0%

commit v1 on v0

v1 whole, which is shorter than its diff:
```python
import jax
import jax.numpy as jnp
from jax import lax
from jax.experimental import pallas as pl
from jax.experimental.pallas import tpu as pltpu
from jax.sharding import PartitionSpec as P

D = 8192
GROUP = 16
TAPS = 7
FILTERS = 512
TOKENS = 1024
WIDTH = 512
ROWS = 64
CHUNK = 256
CHUNKS = TOKENS // CHUNK
MESH = pl.DeviceIdType.MESH

ROUND_ROWS = (3, 0, 1, 2)


def device(x, y, z, core):
    return ((y % 2) * 4 + z, x * 4 + (y // 2) * 2 + core)


def kernel(hidden, weights, bank, assigned, out, hbuf, wbuf, acc, prod, stage, taps, bank8,
           hsem, wsem, sibsem, misc, send):
    seq, chan = lax.axis_index("seq"), lax.axis_index("chan")
    x, y, z, core = chan // 4, (chan // 2 % 2) * 2 + seq // 4, seq % 4, chan % 2
    y_hi, y_lo = y // 2, y % 2
    across = (y_lo + core) % 2
    left, right = (x + 3) % 4, (x + 1) % 4
    down, up = (y + 3) % 4, (y + 1) % 4
    below, above = (z + 3) % 4, (z + 1) % 4
    sibling = device(x, y, z, 1 - core)
    partner = device(x, y + 1 - 2 * y_lo, z, 1 - core)
    x_to = {1: device(right, y, z, core), -1: device(left, y, z, core)}
    y_to = {1: device(x, up, z, core), -1: device(x, down, z, core)}
    z_to = {1: device(x, y, above, core), -1: device(x, y, below, core)}

    def xor(a, bits):
        low, high = a % 2, a // 2
        low = 1 - low if bits & 1 else low
        high = 1 - high if bits & 2 else high
        return high * 2 + low

    mates = []
    for i in range(16):
        mates.append((xor(x, i & 3), xor(y, ((i >> 2) & 1) * 2 + (i >> 3))))

    def copy(src, dst, send_sem, recv_sem, to):
        return pltpu.make_async_remote_copy(
            src_ref=src, dst_ref=dst, send_sem=send_sem, recv_sem=recv_sem,
            device_id=to, device_id_type=MESH)

    def rows_of(piece, owner):
        return pl.ds(pl.multiple_of((piece * 2 + owner) * ROWS, ROWS), ROWS)

    def piece_of(xs, ys, zs):
        return ((ys % 2) * 4 + zs) * 8 + xs * 2 + ys // 2

    def w_send(piece, to, sem):
        ref = wbuf.at[:, rows_of(piece, core), :]
        copy(ref, ref, send.at[sem], wsem.at[piece], to).start()

    def w_sib(piece, group):
        ref = wbuf.at[:, rows_of(piece, core), :]
        copy(ref, ref, send.at[2], sibsem.at[group], sibling).start()

    def w_wait(piece):
        ref = wbuf.at[:, rows_of(piece, core), :]
        copy(ref, ref, send.at[0], wsem.at[piece], sibling).wait_recv()

    def sib_wait(group):
        ref = wbuf.at[:, pl.ds(0, 8 * ROWS), :]
        copy(ref, ref, send.at[2], sibsem.at[group], sibling).wait_recv()

    def block(xs, yh, ks):
        return xs * 4 + yh * 2 + ks

    def h_ref(b, r):
        return hbuf.at[b, pl.ds(ROUND_ROWS[r] * CHUNK, CHUNK), :]

    def h_send(b, r, to, sem):
        copy(h_ref(b, r), h_ref(b, r), send.at[sem], hsem.at[b * CHUNKS + r], to).start()

    def h_x(b, r, sides=(1, -1)):
        for side in sides:
            h_send(b, r, x_to[side], 3)

    def h_y(b, r, sides=(1, -1)):
        for side in sides:
            h_send(b, r, y_to[side], 4)

    def h_wait(b, r):
        copy(h_ref(b, r), h_ref(b, r), send.at[3], hsem.at[b * CHUNKS + r], sibling).wait_recv()

    own_block = block(x, y_hi, core)
    own_piece = piece_of(x, y, z)
    my_group = x * 4 + y

    def local_hidden(r):
        rows = pl.ds(ROUND_ROWS[r] * CHUNK, CHUNK)
        return pltpu.make_async_copy(hidden.at[rows, :], h_ref(own_block, r),
                                     hsem.at[own_block * CHUNKS + r])

    def local_weights(part):
        return pltpu.make_async_copy(
            weights.at[:, pl.ds(pl.multiple_of(part * D + my_group * WIDTH, WIDTH), WIDTH)],
            wbuf.at[part, rows_of(own_piece, core), :], misc.at[2 + part])

    for part in range(3):
        local_weights(part).start()

    @pl.when(across == 0)
    def _():
        for r in range(CHUNKS):
            local_hidden(r).start()

    barrier = pltpu.get_barrier_semaphore()
    greeted = [device(mx, my, z, core) for mx, my in mates[1:]]
    greeted += [z_to[1], z_to[-1], sibling, partner,
                device(x, y, above, 1 - core), device(x, y, below, 1 - core)]
    for to in greeted:
        pl.semaphore_signal(barrier, inc=1, device_id=to, device_id_type=MESH)
    pl.semaphore_wait(barrier, len(greeted))

    def all_to_all(i):
        mx, my = mates[i]
        to = device(mx, my, z, core)
        for part in range(3):
            column = pl.multiple_of(part * D + (mx * 4 + my) * WIDTH, WIDTH)
            copy(weights.at[:, pl.ds(column, WIDTH)], wbuf.at[part, rows_of(own_piece, core), :],
                 send.at[0], wsem.at[own_piece], to).start()

    @pl.when(across == 1)
    def _():
        for r in range(CHUNKS):
            rows = pl.ds(ROUND_ROWS[r] * CHUNK, CHUNK)
            copy(hidden.at[rows, :], h_ref(own_block, r), send.at[5],
                 hsem.at[own_block * CHUNKS + r], sibling).start()

    for i in range(1, 16):
        all_to_all(i)

    def own_weights(i):
        mx, my = mates[i]
        piece = piece_of(mx, my, z)
        if i == 0:
            for part in range(3):
                local_weights(part).wait()
        else:
            w_wait(piece)
        w_send(piece, z_to[1], 1)
        w_send(piece, z_to[-1], 1)
        w_sib(piece, i >> 3)

    def near_weights(i):
        mx, my = mates[i]
        piece = piece_of(mx, my, below)
        w_wait(piece)
        if i % 2 == 0:
            w_send(piece, z_to[1], 1)
        w_sib(piece, 2 + (i >> 3))
        piece = piece_of(mx, my, above)
        w_wait(piece)
        if i % 2 == 1:
            w_send(piece, z_to[-1], 1)
        w_sib(piece, 4 + (i >> 3))

    def far_weights(i):
        mx, my = mates[i]
        piece = piece_of(mx, my, (z + 2) % 4)
        w_wait(piece)
        w_sib(piece, 6 + (i >> 3))

    yh_down, yh_up = down // 2, up // 2

    def hidden0(r):
        @pl.when(across == 0)
        def _():
            a, b = block(x, y_hi, 0), block(x, y_hi, 1)
            h_wait(a, r)
            h_x(a, r)
            h_y(a, r)
            h_wait(b, r)
            h_y(b, r)
            h_x(b, r)

    def hidden1(r):
        @pl.when(across == 0)
        def _():
            a = block(left, y_hi, 0)
            h_wait(a, r)
            if r % 2 == 0:
                h_x(a, r, (1,))
            h_y(a, r)
            a = block(right, y_hi, 0)
            h_wait(a, r)
            if r % 2 == 1:
                h_x(a, r, (-1,))
            h_y(a, r)

        @pl.when(across == 1)
        def _():
            b = block(x, yh_down, 1)
            h_wait(b, r)
            if r % 2 == 0:
                h_y(b, r, (1,))
            h_x(b, r)
            b = block(x, yh_up, 1)
            h_wait(b, r)
            if r % 2 == 1:
                h_y(b, r, (-1,))
            h_x(b, r)

    def hidden2(r):
        @pl.when(across == 0)
        def _():
            a = block((x + 2) % 4, y_hi, 0)
            h_wait(a, r)
            h_y(a, r)
            b = block(x, 1 - y_hi, 1)
            h_wait(b, r)
            h_x(b, r)

    def hidden3(r):
        @pl.when(across == 1)
        def _():
            for m, xs in enumerate((x, left, right, (x + 2) % 4)):
                a = block(xs, yh_down, 0)
                h_wait(a, r)
                if (m + r) % 2 == 0:
                    h_y(a, r, (1,))
                a = block(xs, yh_up, 0)
                h_wait(a, r)
                if (m + r) % 2 == 1:
                    h_y(a, r, (-1,))

        for yh in range(2):
            b = block(left, yh, 1)
            h_wait(b, r)
            if (yh + r) % 2 == 0:
                h_x(b, r, (1,))
            b = block(right, yh, 1)
            h_wait(b, r)
            if (yh + r) % 2 == 1:
                h_x(b, r, (-1,))

    def hidden4(r):
        @pl.when(across == 0)
        def _():
            for xs in (x, left, right, (x + 2) % 4):
                h_wait(block(xs, 1 - y_hi, 0), r)

        for yh in range(2):
            h_wait(block((x + 2) % 4, yh, 1), r)

    def make_taps():
        bank8[0:TAPS, :] = bank[...]
        bank8[TAPS:, :] = jnp.zeros((8 - TAPS, FILTERS), jnp.float32)

        @pl.when(across == 0)
        def _():
            filters = lax.broadcasted_iota(jnp.int32, (FILTERS, WIDTH), 0)
            selector = (filters == assigned[...]).astype(jnp.float32)
            taps[...] = jnp.dot(bank8[...], selector, precision=lax.Precision.HIGHEST,
                                preferred_element_type=jnp.float32)
            copy(taps, taps, send.at[6], misc.at[0], sibling).start()

        @pl.when(across == 1)
        def _():
            copy(taps, taps, send.at[6], misc.at[0], sibling).wait_recv()

        prod[0:8, :] = jnp.zeros((8, WIDTH), jnp.float32)

    def dot(s):
        m = jnp.where(s < 12, s % 6, jnp.where(s < 16, s % 2, s % 8))
        r = jnp.where(s < 12, s // 6, jnp.where(s < 16, (s - 12) // 2, s // 8))
        hop = m // 2
        hop = jnp.where(s < 12, hop + hop // 2, 2)
        z_block = ((y_lo + m) % 2) * 4 + (z + hop) % 4
        step = m // 2
        step = jnp.where(step == 2, 3, jnp.where(step == 3, 2, step))
        x_block = ((x + step) % 4) * 2 + m % 2
        b = jnp.where(s < 16, z_block, x_block)
        rows = jnp.where(r == 0, 3, r - 1) * CHUNK
        rows = pl.ds(pl.multiple_of(rows, CHUNK), CHUNK)
        k0 = pl.ds(pl.multiple_of(b * 1024, 1024), 512)
        k1 = pl.ds(pl.multiple_of(b * 1024 + 512, 512), 512)
        for part in range(3):
            term = jnp.dot(hbuf[2 * b, rows, :], wbuf[part, k0, :],
                           preferred_element_type=jnp.float32)
            term += jnp.dot(hbuf[2 * b + 1, rows, :], wbuf[part, k1, :],
                            preferred_element_type=jnp.float32)
            acc[rows, part * WIDTH:(part + 1) * WIDTH] += term

    SUB = 32

    def products(base):
        def step(i, _):
            rows = pl.ds(pl.multiple_of(base + i * SUB, SUB), SUB)
            prod[pl.ds(pl.multiple_of(base + i * SUB + 8, 8), SUB), :] = (
                acc[rows, WIDTH:2 * WIDTH] * acc[rows, 2 * WIDTH:])
            return 0
        lax.fori_loop(0, CHUNK // SUB, step, 0)

    def filtered(base, count, size):
        def step(i, _):
            first = pl.multiple_of(base + i * size, size)
            near = prod[pl.ds(first, size + 8), :]
            total = jnp.zeros((size, WIDTH), jnp.float32)
            for j in range(TAPS):
                total = total + taps[j:j + 1, :] * near[8 - j:8 - j + size, :]
            rows = pl.ds(first, size)
            stage[rows, :] = (acc[rows, 0:WIDTH] * total).astype(jnp.bfloat16)
            return 0
        lax.fori_loop(0, count, step, 0)

    def out_send(first, count, sem):
        src, dst = stage.at[pl.ds(first, count), :], out.at[pl.ds(first, count), :]

        @pl.when(across == 0)
        def _():
            pltpu.make_async_copy(src, dst, misc.at[sem]).start()

        @pl.when(across == 1)
        def _():
            copy(src, dst, send.at[8], misc.at[sem], partner).start()

    def out_wait(first, count, sem):
        src, dst = stage.at[pl.ds(first, count), :], out.at[pl.ds(first, count), :]

        @pl.when(across == 0)
        def _():
            pltpu.make_async_copy(src, dst, misc.at[sem]).wait()

        @pl.when(across == 1)
        def _():
            copy(src, dst, send.at[8], misc.at[sem], partner).wait_recv()

    halo_from, halo_to = prod.at[pl.ds(TOKENS, 8), :], prod.at[pl.ds(0, 8), :]
    last_window = (z == 3) & (core == 1)
    first_window = (z == 0) & (core == 0)
    next_core = jnp.where(z == 3, 1 - core, core)

    def halo():
        return copy(halo_from, halo_to, send.at[7], misc.at[1], device(x, y, above, next_core))

    def epilogue0():
        products(3 * CHUNK)

        @pl.when(jnp.logical_not(last_window))
        def _():
            halo().start()

        filtered(3 * CHUNK + 32, 7, 32)
        out_send(3 * CHUNK + 32, CHUNK - 32, 5)

    def epilogue1():
        products(0)

        @pl.when(jnp.logical_not(first_window))
        def _():
            halo().wait_recv()

        filtered(0, 8, 32)
        out_send(0, CHUNK, 6)

    def epilogue2():
        products(CHUNK)
        filtered(CHUNK, 8, 32)
        out_send(CHUNK, CHUNK, 7)

    def epilogue3():
        products(2 * CHUNK)
        filtered(2 * CHUNK, 9, 32)
        out_send(2 * CHUNK, CHUNK + 32, 8)

    when, run = {}, {}

    def plan(key, time, fn):
        when[key], run[key] = time, fn

    plan("taps", 3.0, make_taps)
    for i in range(16):
        plan(("own", i), 4 + 3.2 * i, lambda i=i: own_weights(i))
        plan(("near", i), max(50, 10 + 4.2 * i), lambda i=i: near_weights(i))
        plan(("far", i), 70 + 4.2 * (i // 2 + 1), lambda i=i: far_weights(i))
    for r in range(CHUNKS):
        for index, (offset, fn) in enumerate(
                ((0, hidden0), (8, hidden1), (14, hidden2), (20, hidden3), (28, hidden4))):
            plan(("hidden", index, r), 8 + 23 * r + offset, lambda fn=fn, r=r: fn(r))
    for group in range(8):
        members = [("own", "near", "near", "far")[group // 2]]
        last = max(when[members[0], i] for i in range(8 * (group % 2), 8 * (group % 2) + 8))
        plan(("sib", group), last + 4, lambda group=group: sib_wait(group))

    def needs(s):
        r = s // 6 if s < 12 else (s - 12) // 2 if s < 16 else s // 8
        keys = [("hidden", index, r) for index in range(5)]
        if s < 12:
            kinds = [(("own", 0), ("near", 4), ("near", 2))[s % 6 // 2]]
            halves = [s % 2]
        else:
            kinds = [("own", 0), ("near", 4), ("near", 2), ("far", 6)]
            halves = [0, 1]
        for kind, group in kinds:
            for half in halves:
                keys += [(kind, i) for i in range(8 * half, 8 * half + 8)]
                keys.append(("sib", group + half))
        return keys

    before = [[] for _ in range(32)]
    placed = set()
    clock = 0.0
    for s in range(32):
        clock = max([clock + 1.25] + [when[key] for key in needs(s)])
        ready = [key for key in when if when[key] <= clock and key not in placed]
        for key in sorted(ready, key=when.get):
            placed.add(key)
            before[s].append(run[key])
        if s in (16, 17, 24):
            before[s].append({16: epilogue0, 17: epilogue1, 24: epilogue2}[s])
    assert len(placed) == len(when)

    def zero(i, _):
        acc[pl.ds(pl.multiple_of(i * 32, 32), 32), :] = jnp.zeros((32, 3 * WIDTH), jnp.float32)
        return 0
    lax.fori_loop(0, TOKENS // 32, zero, 0)

    def slot_step(s, _):
        for k in range(32):
            if before[k]:
                @pl.when(s == k)
                def _(k=k):
                    for fn in before[k]:
                        fn()
        dot(s)
        return 0
    lax.fori_loop(0, 32, slot_step, 0)
    epilogue3()

    out_wait(3 * CHUNK + 32, CHUNK - 32, 5)
    out_wait(0, CHUNK, 6)
    out_wait(CHUNK, CHUNK, 7)
    out_wait(2 * CHUNK, CHUNK + 32, 8)

    def sent(ref, sem):
        copy(ref, ref, send.at[sem], misc.at[0], sibling).wait_send()

    sent(wbuf.at[:, pl.ds(0, 15 * ROWS), :], 0)
    sent(wbuf.at[:, pl.ds(0, 48 * ROWS), :], 1)
    sent(wbuf.at[:, pl.ds(0, 64 * ROWS), :], 2)

    @pl.when(across == 0)
    def _():
        sent(hbuf.at[pl.ds(0, 9)], 3)
        sent(hbuf.at[pl.ds(0, 10)], 4)
        sent(taps, 6)

    @pl.when(across == 1)
    def _():
        sent(hbuf.at[pl.ds(0, 6)], 3)
        sent(hbuf.at[pl.ds(0, 5)], 4)
        sent(hidden, 5)
        sent(stage, 8)

    @pl.when(jnp.logical_not(last_window))
    def _():
        halo().wait_send()


def on_device(hidden, in_weights, filter_bank, assignment):
    assigned = jnp.repeat(assignment, GROUP)[None, :]
    any_space = pl.BlockSpec(memory_space=pl.ANY)
    vmem = pl.BlockSpec(memory_space=pltpu.VMEM)
    return pl.pallas_call(
        kernel,
        name="hyena",
        out_shape=jax.ShapeDtypeStruct((TOKENS, WIDTH), jnp.bfloat16),
        in_specs=[any_space, any_space, vmem, vmem],
        out_specs=any_space,
        scratch_shapes=[
            pltpu.VMEM((16, TOKENS, WIDTH), jnp.bfloat16),
            pltpu.VMEM((3, D, WIDTH), jnp.bfloat16),
            pltpu.VMEM((TOKENS, 3 * WIDTH), jnp.float32),
            pltpu.VMEM((TOKENS + 8, WIDTH), jnp.float32),
            pltpu.VMEM((TOKENS, WIDTH), jnp.bfloat16),
            pltpu.VMEM((8, WIDTH), jnp.float32),
            pltpu.VMEM((8, FILTERS), jnp.float32),
            pltpu.SemaphoreType.DMA((16 * CHUNKS,)),
            pltpu.SemaphoreType.DMA((64,)),
            pltpu.SemaphoreType.DMA((8,)),
            pltpu.SemaphoreType.DMA((9,)),
            pltpu.SemaphoreType.DMA((9,)),
        ],
        compiler_params=pltpu.CompilerParams(
            collective_id=0, has_side_effects=True, vmem_limit_bytes=60 * 2**20),
        cost_estimate=pl.CostEstimate(
            flops=2 * TOKENS * D * 3 * WIDTH, bytes_accessed=44 * 2**20, transcendentals=0),
    )(hidden, in_weights, filter_bank, assigned)


def solution(mesh):
    in_specs = (P("seq", "chan"), P(("seq", "chan"), None), P(), P("chan"))
    return jax.shard_map(
        on_device, mesh=mesh, in_specs=in_specs, out_specs=P("seq", "chan"), check_vma=False)
```

time: 469 us -> 210 us (0.45)
  waiting for transfers between devices: 339 us -> 0 us
  Pallas kernels: 0 us -> 206 us
  blocking collectives: 59.4 us -> 0 us
  matrix products: 32.8 us -> 0 us
  between operations: 13.5 us -> 0.01 us
  local copies, waits for them, and re-layouts: 13.4 us -> 3.65 us
  other arithmetic: 5.87 us -> 0 us
    all_gather x2 -> x0, waiting for transfers between devices: 334 us -> none  [the longest x1 249 us: on_device(): lax.all_gather(regrouped, 'seq', axis=0, tiled=True)]
    pallas_call x0 -> x1, Pallas kernels: none -> 206 us  [on_device(): pl.pallas_call(kernel, name='hyena', out_shape=jax.ShapeDtypeStruct((TOKE...]
    all_to_all x1 -> x0, blocking collectives: 59.4 us -> none  [on_device(): lax.all_to_all(sectioned, 'chan', split_axis=2, concat_axis=0, tiled=True)]
    dot_general x2 -> x0, matrix products: 32.8 us -> none  [the longest x1 32.6 us: on_device(): jnp.dot(widened, lax.all_gather(regrouped, 'seq', axis=0, tiled=True), pr...]
    convert_element_type x1 -> x0, other arithmetic: 4.77 us -> none  [on_device(): return (query_part * filtered).astype(jnp.bfloat16)]
    ppermute x1 -> x0, waiting for transfers between devices: 4.7 us -> none  [shifted(): return lax.ppermute(block, axis, route)]
  transfers between devices with their start and end apart: 3 -> 0, of which waited for: 3 -> 0; matrix products, arithmetic and copies ran while one was open for 3% -> 0% of each run, Pallas kernels for 0% -> 0%
where the time goes in v1:
time: 210 us
  Pallas kernels  206 us (98%)
  local copies, waits for them, and re-layouts  3.65 us (2%)
    pallas_call x1, Pallas kernels, on_device(): pl.pallas_call(kernel, name='hyena', out_shape=jax.ShapeDtypeStruct((TOKE...  206 us

profile of v1, /device:TPU:1, one launch (start us, length us, event | category | flops | bytes accessed | tf_op | source)
XLA Modules:
  0.0 209.8 jit_solution(18009204256583718979)
XLA Ops:
  0.0 0.7 broadcast_in_dim.3
  0.7 0.7 broadcast_in_dim_reshape.3.assigned
  1.4 206.1 %hyena.1 = bf16[1024,512]{1,0:T(8,128)(2,1)} custom-call(bf16[1024,512]{1,0:T(8,128)(2,1)} %hidden.1, bf16[64,24576]{1,0:T(8,128)(2,1)} %weights.1, f32[7,512]{1,0:T(8,128)} %bank.1, s32[1,512]{1,0:T(1,128)} %broadcast_in_dim_reshape.3.assigned), custom_call_target="tpu_custom_call" | custom-call | flops 25769803776 | bytes 46137344 | tf_op jit(solution)/shard_map/hyena/pallas_call | solution.py:478
  207.5 2.3 %copy.6 = bf16[1024,512]{1,0:T(8,128)(2,1)} copy(bf16[1024,512]{1,0:T(8,128)(2,1)} %hyena.1) | data formatting | bytes 2097152

commit v2 on v1

--- a/solution.py
+++ b/solution.py
@@ -17,6 +17,71 @@
 MESH = pl.DeviceIdType.MESH
 
 ROUND_ROWS = (3, 0, 1, 2)
+ORDER = ((0, 0), (1, 0), (3, 0), (0, 2), (2, 0), (1, 2), (3, 2), (2, 2),
+         (0, 1), (0, 3), (1, 1), (3, 3), (1, 3), (3, 1), (2, 1), (2, 3))
+FIRST, AFTER = 8.0, 16.0
+STAGES = (0.0, 12.0, 24.0, 36.0, 50.0)
+LAST = (0.0, 12.0, 24.0, 36.0, 50.0)
+SPREAD = (0.1, 0.1)
+SPLIT = 6.0
+ALL = (3.0, 0.5)
+OWN = (4.0, 3.2)
+NEAR = (50.0, 10.0, 4.2)
+FAR = (70.0, 4.2)
+DOT = 1.25
+
+HOPS = (0, 1, 3, 2)
+DOTS = tuple(("z", r, hop, half) for r in range(3) for hop in HOPS[:3] for half in range(2))
+DOTS += tuple(("z", r, 2, half) for half in range(2) for r in range(3))
+DOTS += tuple(("x", 3, step, y_hi) for step in range(4) for y_hi in range(2))
+
+
+def hidden_needs(m, r):
+    return [("h3a", m, r), ("h4a", m, r)] + [
+        [("h1", r), ("h2", r)], [("h1", r), ("h3b", r)], [("h1", r), ("h3b", r)],
+        [("h2", r), ("h4b", r)]][m]
+
+
+def timeline():
+    when = {("taps",): 30.0, ("zero",): 33.0}
+    for i in range(16):
+        if i:
+            when["all", i] = ALL[0] + ALL[1] * i
+        when["own", i] = OWN[0] + OWN[1] * i
+        when["near", i] = max(NEAR[0], NEAR[1] + NEAR[2] * i)
+        when["far", i] = FAR[0] + FAR[1] * (i // 2 + 1)
+    for r in range(CHUNKS):
+        start = FIRST + AFTER * r
+        stages = STAGES if r < CHUNKS - 1 else LAST
+        when["h0b", r] = start + stages[0] + SPLIT
+        for index in range(3):
+            when["h%d" % index, r] = start + stages[index]
+        for m in range(4):
+            when["h3a", m, r] = start + stages[3] + SPREAD[0] * m
+            when["h4a", m, r] = start + stages[4] + SPREAD[1] * m
+        when["h3b", r] = start + stages[3] + SPREAD[0] * 1.5
+        when["h4b", r] = start + stages[4] + SPREAD[1] * 2.5
+    kinds = {0: "own", 1: "near", 3: "near", 2: "far"}
+    for hop in HOPS:
+        for half in range(2):
+            last = max(when[kinds[hop], i] for i in range(16) if ORDER[i][1] % 2 == half)
+            when["sib", hop, half] = last + 3.0
+
+    slots, placed, clock = [], set(), 0.0
+    names = list(when)
+    for kind, r, step, half in DOTS:
+        if kind == "z":
+            needs = [key for m in range(4) for key in hidden_needs(m, r)] + [("sib", step, half)]
+        else:
+            needs = hidden_needs(step, r) + [("sib", hop, h) for hop in HOPS for h in range(2)]
+        clock = max([clock + DOT] + [when[key] for key in needs])
+        ready = [key for key in names if when[key] <= clock and key not in placed]
+        ready = sorted(ready, key=when.get)
+        placed.update(ready)
+        slots.append(ready)
+    rest = [key for key in names if key not in placed]
+    assert not rest
+    return slots
 
 
 def device(x, y, z, core):
@@ -38,15 +103,9 @@
     y_to = {1: device(x, up, z, core), -1: device(x, down, z, core)}
     z_to = {1: device(x, y, above, core), -1: device(x, y, below, core)}
 
-    def xor(a, bits):
-        low, high = a % 2, a // 2
-        low = 1 - low if bits & 1 else low
-        high = 1 - high if bits & 2 else high
-        return high * 2 + low
-
-    mates = []
-    for i in range(16):
-        mates.append((xor(x, i & 3), xor(y, ((i >> 2) & 1) * 2 + (i >> 3))))
+    sign = 1 - 2 * core
+    mates_to = [((x + sign * dx + 4) % 4, (y + sign * dy + 4) % 4) for dx, dy in ORDER]
+    mates = [((x - sign * dx + 4) % 4, (y - sign * dy + 4) % 4) for dx, dy in ORDER]
 
     def copy(src, dst, send_sem, recv_sem, to):
         return pltpu.make_async_remote_copy(
@@ -71,9 +130,9 @@
         ref = wbuf.at[:, rows_of(piece, core), :]
         copy(ref, ref, send.at[0], wsem.at[piece], sibling).wait_recv()
 
-    def sib_wait(group):
+    def sib_wait(hop, half):
         ref = wbuf.at[:, pl.ds(0, 8 * ROWS), :]
-        copy(ref, ref, send.at[2], sibsem.at[group], sibling).wait_recv()
+        copy(ref, ref, send.at[2], sibsem.at[2 * hop + half], sibling).wait_recv()
 
     def block(xs, yh, ks):
         return xs * 4 + yh * 2 + ks
@@ -118,7 +177,7 @@
             local_hidden(r).start()
 
     barrier = pltpu.get_barrier_semaphore()
-    greeted = [device(mx, my, z, core) for mx, my in mates[1:]]
+    greeted = [device(mx, my, z, core) for mx, my in mates_to[1:]]
     greeted += [z_to[1], z_to[-1], sibling, partner,
                 device(x, y, above, 1 - core), device(x, y, below, 1 - core)]
     for to in greeted:
@@ -126,12 +185,11 @@
     pl.semaphore_wait(barrier, len(greeted))
 
     def all_to_all(i):
-        mx, my = mates[i]
-        to = device(mx, my, z, core)
+        mx, my = mates_to[i]
         for part in range(3):
-            column = pl.multiple_of(part * D + (mx * 4 + my) * WIDTH, WIDTH)
-            copy(weights.at[:, pl.ds(column, WIDTH)], wbuf.at[part, rows_of(own_piece, core), :],
-                 send.at[0], wsem.at[own_piece], to).start()
+            columns = pl.ds(pl.multiple_of(part * D + (mx * 4 + my) * WIDTH, WIDTH), WIDTH)
+            copy(weights.at[:, columns], wbuf.at[part, rows_of(own_piece, core), :],
+                 send.at[0], wsem.at[own_piece], device(mx, my, z, core)).start()
 
     @pl.when(across == 1)
     def _():
@@ -139,9 +197,6 @@
             rows = pl.ds(ROUND_ROWS[r] * CHUNK, CHUNK)
             copy(hidden.at[rows, :], h_ref(own_block, r), send.at[5],
                  hsem.at[own_block * CHUNKS + r], sibling).start()
-
-    for i in range(1, 16):
-        all_to_all(i)
 
     def own_weights(i):
         mx, my = mates[i]
@@ -153,7 +208,7 @@
             w_wait(piece)
         w_send(piece, z_to[1], 1)
         w_send(piece, z_to[-1], 1)
-        w_sib(piece, i >> 3)
+        w_sib(piece, ORDER[i][1] % 2)
 
     def near_weights(i):
         mx, my = mates[i]
@@ -161,18 +216,18 @@
         w_wait(piece)
         if i % 2 == 0:
             w_send(piece, z_to[1], 1)
-        w_sib(piece, 2 + (i >> 3))
+        w_sib(piece, 6 + ORDER[i][1] % 2)
         piece = piece_of(mx, my, above)
         w_wait(piece)
         if i % 2 == 1:
             w_send(piece, z_to[-1], 1)
-        w_sib(piece, 4 + (i >> 3))
+        w_sib(piece, 2 + ORDER[i][1] % 2)
 
     def far_weights(i):
         mx, my = mates[i]
         piece = piece_of(mx, my, (z + 2) % 4)
         w_wait(piece)
-        w_sib(piece, 6 + (i >> 3))
+        w_sib(piece, 4 + ORDER[i][1] % 2)
 
     yh_down, yh_up = down // 2, up // 2
 
@@ -182,10 +237,14 @@
             a, b = block(x, y_hi, 0), block(x, y_hi, 1)
             h_wait(a, r)
             h_x(a, r)
-            h_y(a, r)
             h_wait(b, r)
             h_y(b, r)
-            h_x(b, r)
+
+    def hidden0b(r):
+        @pl.when(across == 0)
+        def _():
+            h_y(block(x, y_hi, 0), r)
+            h_x(block(x, y_hi, 1), r)
 
     def hidden1(r):
         @pl.when(across == 0)
@@ -224,19 +283,21 @@
             h_wait(b, r)
             h_x(b, r)
 
-    def hidden3(r):
+    xs_steps = (x, left, right, (x + 2) % 4)
+
+    def hidden3a(m, r):
         @pl.when(across == 1)
         def _():
-            for m, xs in enumerate((x, left, right, (x + 2) % 4)):
-                a = block(xs, yh_down, 0)
-                h_wait(a, r)
-                if (m + r) % 2 == 0:
-                    h_y(a, r, (1,))
-                a = block(xs, yh_up, 0)
-                h_wait(a, r)
-                if (m + r) % 2 == 1:
-                    h_y(a, r, (-1,))
-
+            a = block(xs_steps[m], yh_down, 0)
+            h_wait(a, r)
+            if (m + r) % 2 == 0:
+                h_y(a, r, (1,))
+            a = block(xs_steps[m], yh_up, 0)
+            h_wait(a, r)
+            if (m + r) % 2 == 1:
+                h_y(a, r, (-1,))
+
+    def hidden3b(r):
         for yh in range(2):
             b = block(left, yh, 1)
             h_wait(b, r)
@@ -247,12 +308,12 @@
             if (yh + r) % 2 == 1:
                 h_x(b, r, (-1,))
 
-    def hidden4(r):
-        @pl.when(across == 0)
-        def _():
-            for xs in (x, left, right, (x + 2) % 4):
-                h_wait(block(xs, 1 - y_hi, 0), r)
-
+    def hidden4a(m, r):
+        @pl.when(across == 0)
+        def _():
+            h_wait(block(xs_steps[m], 1 - y_hi, 0), r)
+
+    def hidden4b(r):
         for yh in range(2):
             h_wait(block((x + 2) % 4, yh, 1), r)
 
@@ -274,26 +335,26 @@
 
         prod[0:8, :] = jnp.zeros((8, WIDTH), jnp.float32)
 
+    codes = [(kind == "x") * 32 + r * 8 + step * 2 + half for kind, r, step, half in DOTS]
+    words = [sum(code << 6 * i for i, code in enumerate(codes[first:first + 5]))
+             for first in range(0, len(codes), 5)]
+
     def dot(s):
-        m = jnp.where(s < 12, s % 6, jnp.where(s < 16, s % 2, s % 8))
-        r = jnp.where(s < 12, s // 6, jnp.where(s < 16, (s - 12) // 2, s // 8))
-        hop = m // 2
-        hop = jnp.where(s < 12, hop + hop // 2, 2)
-        z_block = ((y_lo + m) % 2) * 4 + (z + hop) % 4
-        step = m // 2
-        step = jnp.where(step == 2, 3, jnp.where(step == 3, 2, step))
-        x_block = ((x + step) % 4) * 2 + m % 2
-        b = jnp.where(s < 16, z_block, x_block)
-        rows = jnp.where(r == 0, 3, r - 1) * CHUNK
-        rows = pl.ds(pl.multiple_of(rows, CHUNK), CHUNK)
-        k0 = pl.ds(pl.multiple_of(b * 1024, 1024), 512)
-        k1 = pl.ds(pl.multiple_of(b * 1024 + 512, 512), 512)
+        word = jnp.int32(words[0])
+        for i in range(1, len(words)):
+            word = jnp.where(s >= 5 * i, jnp.int32(words[i]), word)
+        code = lax.shift_right_logical(word, 6 * (s % 5)) % 64
+        by_x, r, step, half = code // 32, code // 8 % 4, code // 2 % 4, code % 2
+        z_block = ((y_lo + half) % 2) * 4 + (z + step) % 4
+        shift = jnp.where(step == 0, 0, jnp.where(step == 1, 3, step - 1))
+        x_block = ((x + shift) % 4) * 2 + half
+        b = jnp.where(by_x == 1, x_block, z_block)
+        rows = pl.ds(pl.multiple_of((r + 3) % 4 * CHUNK, CHUNK), CHUNK)
+        depth = pl.ds(pl.multiple_of(b * 1024, 1024), 1024)
+        left_side = jnp.concatenate([hbuf[2 * b, rows, :], hbuf[2 * b + 1, rows, :]], axis=1)
         for part in range(3):
-            term = jnp.dot(hbuf[2 * b, rows, :], wbuf[part, k0, :],
-                           preferred_element_type=jnp.float32)
-            term += jnp.dot(hbuf[2 * b + 1, rows, :], wbuf[part, k1, :],
-                            preferred_element_type=jnp.float32)
-            acc[rows, part * WIDTH:(part + 1) * WIDTH] += term
+            acc[rows, part * WIDTH:(part + 1) * WIDTH] += jnp.dot(
+                left_side, wbuf[part, depth, :], preferred_element_type=jnp.float32)
 
     SUB = 32
 
@@ -377,68 +438,31 @@
         filtered(2 * CHUNK, 9, 32)
         out_send(2 * CHUNK, CHUNK + 32, 8)
 
-    when, run = {}, {}
-
-    def plan(key, time, fn):
-        when[key], run[key] = time, fn
-
-    plan("taps", 3.0, make_taps)
-    for i in range(16):
-        plan(("own", i), 4 + 3.2 * i, lambda i=i: own_weights(i))
-        plan(("near", i), max(50, 10 + 4.2 * i), lambda i=i: near_weights(i))
-        plan(("far", i), 70 + 4.2 * (i // 2 + 1), lambda i=i: far_weights(i))
-    for r in range(CHUNKS):
-        for index, (offset, fn) in enumerate(
-                ((0, hidden0), (8, hidden1), (14, hidden2), (20, hidden3), (28, hidden4))):
-            plan(("hidden", index, r), 8 + 23 * r + offset, lambda fn=fn, r=r: fn(r))
-    for group in range(8):
-        members = [("own", "near", "near", "far")[group // 2]]
-        last = max(when[members[0], i] for i in range(8 * (group % 2), 8 * (group % 2) + 8))
-        plan(("sib", group), last + 4, lambda group=group: sib_wait(group))
-
-    def needs(s):
-        r = s // 6 if s < 12 else (s - 12) // 2 if s < 16 else s // 8
-        keys = [("hidden", index, r) for index in range(5)]
-        if s < 12:
-            kinds = [(("own", 0), ("near", 4), ("near", 2))[s % 6 // 2]]
-            halves = [s % 2]
-        else:
-            kinds = [("own", 0), ("near", 4), ("near", 2), ("far", 6)]
-            halves = [0, 1]
-        for kind, group in kinds:
-            for half in halves:
-                keys += [(kind, i) for i in range(8 * half, 8 * half + 8)]
-                keys.append(("sib", group + half))
-        return keys
-
-    before = [[] for _ in range(32)]
-    placed = set()
-    clock = 0.0
-    for s in range(32):
-        clock = max([clock + 1.25] + [when[key] for key in needs(s)])
-        ready = [key for key in when if when[key] <= clock and key not in placed]
-        for key in sorted(ready, key=when.get):
-            placed.add(key)
-            before[s].append(run[key])
-        if s in (16, 17, 24):
-            before[s].append({16: epilogue0, 17: epilogue1, 24: epilogue2}[s])
-    assert len(placed) == len(when)
-
-    def zero(i, _):
-        acc[pl.ds(pl.multiple_of(i * 32, 32), 32), :] = jnp.zeros((32, 3 * WIDTH), jnp.float32)
-        return 0
-    lax.fori_loop(0, TOKENS // 32, zero, 0)
+    def zero_acc():
+        def step(i, _):
+            rows = pl.ds(pl.multiple_of(i * 32, 32), 32)
+            acc[rows, :] = jnp.zeros((32, 3 * WIDTH), jnp.float32)
+            return 0
+        lax.fori_loop(0, TOKENS // 32, step, 0)
+
+    run = {"taps": make_taps, "zero": zero_acc, "all": all_to_all, "own": own_weights, "near": near_weights, "far": far_weights, "sib": sib_wait,
+           "h0": hidden0, "h0b": hidden0b, "h1": hidden1, "h2": hidden2, "h3a": hidden3a, "h3b": hidden3b,
+           "h4a": hidden4a, "h4b": hidden4b}
+    before = timeline()
+    last_dot = {r: max(s for s in range(len(DOTS)) if DOTS[s][1] == r) for r in range(CHUNKS)}
 
     def slot_step(s, _):
-        for k in range(32):
-            if before[k]:
-                @pl.when(s == k)
-                def _(k=k):
-                    for fn in before[k]:
-                        fn()
+        for k in range(len(DOTS)):
+            @pl.when(s == k)
+            def _(k=k):
+                for name, *args in before[k]:
+                    run[name](*args)
+                for r, epilogue in enumerate((epilogue0, epilogue1, epilogue2)):
+                    if k == max(last_dot[i] for i in range(r + 1)) + 1:
+                        epilogue()
         dot(s)
         return 0
-    lax.fori_loop(0, 32, slot_step, 0)
+    lax.fori_loop(0, len(DOTS), slot_step, 0)
     epilogue3()
 
     out_wait(3 * CHUNK + 32, CHUNK - 32, 5)

time: 210 us -> 173 us (0.82)
  Pallas kernels: 206 us -> 169 us
    pallas_call x1, Pallas kernels: 206 us -> 169 us  [on_device(): pl.pallas_call(kernel, name='hyena', out_shape=jax.ShapeDtypeStruct((TOKE...]
where the time goes in v2:
time: 173 us
  Pallas kernels  169 us (98%)
  local copies, waits for them, and re-layouts  3.65 us (2%)
    pallas_call x1, Pallas kernels, on_device(): pl.pallas_call(kernel, name='hyena', out_shape=jax.ShapeDtypeStruct((TOKE...  169 us

profile of v2, /device:TPU:1, one launch (start us, length us, event | category | flops | bytes accessed | tf_op | source)
XLA Modules:
  0.0 172.9 jit_solution(3842262212353330295)
XLA Ops:
  0.0 0.7 broadcast_in_dim.3
  0.7 0.7 broadcast_in_dim_reshape.3.assigned
  1.4 169.3 %hyena.1 = bf16[1024,512]{1,0:T(8,128)(2,1)} custom-call(bf16[1024,512]{1,0:T(8,128)(2,1)} %hidden.1, bf16[64,24576]{1,0:T(8,128)(2,1)} %weights.1, f32[7,512]{1,0:T(8,128)} %bank.1, s32[1,512]{1,0:T(1,128)} %broadcast_in_dim_reshape.3.assigned), custom_call_target="tpu_custom_call" | custom-call | flops 25769803776 | bytes 46137344 | tf_op jit(solution)/shard_map/hyena/pallas_call | solution.py:502
  170.7 2.3 %copy.6 = bf16[1024,512]{1,0:T(8,128)(2,1)} copy(bf16[1024,512]{1,0:T(8,128)(2,1)} %hyena.1) | data formatting | bytes 2097152

commit v3 on v2

--- a/solution.py
+++ b/solution.py
@@ -19,21 +19,28 @@
 ROUND_ROWS = (3, 0, 1, 2)
 ORDER = ((0, 0), (1, 0), (3, 0), (0, 2), (2, 0), (1, 2), (3, 2), (2, 2),
          (0, 1), (0, 3), (1, 1), (3, 3), (1, 3), (3, 1), (2, 1), (2, 3))
-FIRST, AFTER = 8.0, 16.0
-STAGES = (0.0, 12.0, 24.0, 36.0, 50.0)
-LAST = (0.0, 12.0, 24.0, 36.0, 50.0)
-SPREAD = (0.1, 0.1)
-SPLIT = 6.0
-ALL = (3.0, 0.5)
-OWN = (4.0, 3.2)
-NEAR = (50.0, 10.0, 4.2)
-FAR = (70.0, 4.2)
-DOT = 1.25
+FIRST, AFTER = 19.54, 20.63
+STAGES = (0.0, 6.54, 23.09, 34.44, 49.63)
+LAST = (12.84, 25.44, 35.22, 44.3, 71.25)
+SPREAD = (2.51, 2.56)
+SPLIT = 21.05
+ALL = (0, 0.5)
+OWN = (3.64, 1.48)
+NEAR = (19.06, 1.08, 5.8)
+FAR = (73.66, 4.68)
+DOT = 1.7
 
 HOPS = (0, 1, 3, 2)
-DOTS = tuple(("z", r, hop, half) for r in range(3) for hop in HOPS[:3] for half in range(2))
-DOTS += tuple(("z", r, 2, half) for half in range(2) for r in range(3))
-DOTS += tuple(("x", 3, step, y_hi) for step in range(4) for y_hi in range(2))
+DOTS = (
+    ("z", 0, 0, 0), ("z", 0, 1, 0), ("z", 0, 3, 0), ("z", 1, 0, 0),
+    ("z", 1, 1, 0), ("z", 1, 3, 0), ("z", 0, 0, 1), ("z", 0, 1, 1),
+    ("z", 0, 3, 1), ("z", 1, 0, 1), ("z", 1, 1, 1), ("z", 1, 3, 1),
+    ("z", 0, 2, 0), ("z", 1, 2, 0), ("z", 2, 0, 0), ("z", 2, 0, 1),
+    ("z", 2, 1, 0), ("z", 2, 1, 1), ("z", 2, 3, 0), ("z", 2, 3, 1),
+    ("z", 2, 2, 0), ("z", 0, 2, 1), ("z", 1, 2, 1), ("z", 2, 2, 1),
+    ("x", 3, 0, 0), ("x", 3, 0, 1), ("x", 3, 1, 0), ("x", 3, 1, 1),
+    ("x", 3, 2, 0), ("x", 3, 2, 1), ("x", 3, 3, 0), ("x", 3, 3, 1),
+)
 
 
 def hidden_needs(m, r):

time: 173 us -> 164 us (0.948); the launches traced: 173 us -> 162 us
  Pallas kernels: 169 us -> 158 us
    pallas_call x1, Pallas kernels: 169 us -> 158 us  [on_device(): pl.pallas_call(kernel, name='hyena', out_shape=jax.ShapeDtypeStruct((TOKE...]
where the time goes in v3:
time: 164 us; the launch traced here: 162 us
  Pallas kernels  158 us (96%)
  local copies, waits for them, and re-layouts  3.65 us (2%)
    pallas_call x1, Pallas kernels, on_device(): pl.pallas_call(kernel, name='hyena', out_shape=jax.ShapeDtypeStruct((TOKE...  158 us

profile of v3, /device:TPU:1, one launch (start us, length us, event | category | flops | bytes accessed | tf_op | source)
XLA Modules:
  0.0 162.1 jit_solution(4658075676164827107)
XLA Ops:
  0.0 0.7 broadcast_in_dim.3
  0.7 0.7 broadcast_in_dim_reshape.3.assigned
  1.4 158.4 %hyena.1 = bf16[1024,512]{1,0:T(8,128)(2,1)} custom-call(bf16[1024,512]{1,0:T(8,128)(2,1)} %hidden.1, bf16[64,24576]{1,0:T(8,128)(2,1)} %weights.1, f32[7,512]{1,0:T(8,128)} %bank.1, s32[1,512]{1,0:T(1,128)} %broadcast_in_dim_reshape.3.assigned), custom_call_target="tpu_custom_call" | custom-call | flops 25769803776 | bytes 46137344 | tf_op jit(solution)/shard_map/hyena/pallas_call | solution.py:509
  159.8 2.3 %copy.6 = bf16[1024,512]{1,0:T(8,128)(2,1)} copy(bf16[1024,512]{1,0:T(8,128)(2,1)} %hyena.1) | data formatting | bytes 2097152

commit v4 on v3

--- a/solution.py
+++ b/solution.py
@@ -16,10 +16,10 @@
 CHUNKS = TOKENS // CHUNK
 MESH = pl.DeviceIdType.MESH
 
-ROUND_ROWS = (3, 0, 1, 2)
+ROUNDS = ((768, 256), (0, 256), (256, 256), (512, 256))
 ORDER = ((0, 0), (1, 0), (3, 0), (0, 2), (2, 0), (1, 2), (3, 2), (2, 2),
          (0, 1), (0, 3), (1, 1), (3, 3), (1, 3), (3, 1), (2, 1), (2, 3))
-FIRST, AFTER = 19.54, 20.63
+STARTS = (19.54, 40.17, 60.8, 81.43)
 STAGES = (0.0, 6.54, 23.09, 34.44, 49.63)
 LAST = (12.84, 25.44, 35.22, 44.3, 71.25)
 SPREAD = (2.51, 2.56)
@@ -38,7 +38,7 @@
     ("z", 0, 2, 0), ("z", 1, 2, 0), ("z", 2, 0, 0), ("z", 2, 0, 1),
     ("z", 2, 1, 0), ("z", 2, 1, 1), ("z", 2, 3, 0), ("z", 2, 3, 1),
     ("z", 2, 2, 0), ("z", 0, 2, 1), ("z", 1, 2, 1), ("z", 2, 2, 1),
-    ("x", 3, 0, 0), ("x", 3, 0, 1), ("x", 3, 1, 0), ("x", 3, 1, 1),
+    ("x", 3, 0, 1), ("x", 3, 0, 0), ("x", 3, 1, 0), ("x", 3, 1, 1),
     ("x", 3, 2, 0), ("x", 3, 2, 1), ("x", 3, 3, 0), ("x", 3, 3, 1),
 )
 
@@ -57,9 +57,8 @@
         when["own", i] = OWN[0] + OWN[1] * i
         when["near", i] = max(NEAR[0], NEAR[1] + NEAR[2] * i)
         when["far", i] = FAR[0] + FAR[1] * (i // 2 + 1)
-    for r in range(CHUNKS):
-        start = FIRST + AFTER * r
-        stages = STAGES if r < CHUNKS - 1 else LAST
+    for r, start in enumerate(STARTS):
+        stages = LAST if r == CHUNKS - 1 else STAGES
         when["h0b", r] = start + stages[0] + SPLIT
         for index in range(3):
             when["h%d" % index, r] = start + stages[index]
@@ -78,9 +77,11 @@
     names = list(when)
     for kind, r, step, half in DOTS:
         if kind == "z":
-            needs = [key for m in range(4) for key in hidden_needs(m, r)] + [("sib", step, half)]
+            needs = [key for m in range(4) for key in hidden_needs(m, r)]
+            needs += [("sib", step, half)]
         else:
-            needs = hidden_needs(step, r) + [("sib", hop, h) for hop in HOPS for h in range(2)]
+            needs = hidden_needs(step, r) + [
+                ("sib", hop, h) for hop in HOPS for h in range(2)]
         clock = max([clock + DOT] + [when[key] for key in needs])
         ready = [key for key in names if when[key] <= clock and key not in placed]
         ready = sorted(ready, key=when.get)
@@ -145,30 +146,36 @@
         return xs * 4 + yh * 2 + ks
 
     def h_ref(b, r):
-        return hbuf.at[b, pl.ds(ROUND_ROWS[r] * CHUNK, CHUNK), :]
+        return hbuf.at[b, pl.ds(*ROUNDS[r]), :]
+
+    def h_sem(b, r):
+        return hsem.at[b * len(ROUNDS) + r]
 
     def h_send(b, r, to, sem):
-        copy(h_ref(b, r), h_ref(b, r), send.at[sem], hsem.at[b * CHUNKS + r], to).start()
-
-    def h_x(b, r, sides=(1, -1)):
-        for side in sides:
+        copy(h_ref(b, r), h_ref(b, r), send.at[sem], h_sem(b, r), to).start()
+
+    def h_x(b, r):
+        for side in (1, -1):
             h_send(b, r, x_to[side], 3)
 
-    def h_y(b, r, sides=(1, -1)):
-        for side in sides:
+    def h_y(b, r):
+        for side in (1, -1):
             h_send(b, r, y_to[side], 4)
 
+    def pass_on(to, sem, side, b, r):
+        h_send(b, r, to[side], sem)
+
     def h_wait(b, r):
-        copy(h_ref(b, r), h_ref(b, r), send.at[3], hsem.at[b * CHUNKS + r], sibling).wait_recv()
+        copy(h_ref(b, r), h_ref(b, r), send.at[3], h_sem(b, r), sibling).wait_recv()
 
     own_block = block(x, y_hi, core)
     own_piece = piece_of(x, y, z)
     my_group = x * 4 + y
 
     def local_hidden(r):
-        rows = pl.ds(ROUND_ROWS[r] * CHUNK, CHUNK)
+        rows = pl.ds(*ROUNDS[r])
         return pltpu.make_async_copy(hidden.at[rows, :], h_ref(own_block, r),
-                                     hsem.at[own_block * CHUNKS + r])
+                                     h_sem(own_block, r))
 
     def local_weights(part):
         return pltpu.make_async_copy(
@@ -180,8 +187,10 @@
 
     @pl.when(across == 0)
     def _():
-        for r in range(CHUNKS):
+        for r in range(len(ROUNDS)):
             local_hidden(r).start()
+
+    prod[0:8, :] = jnp.zeros((8, WIDTH), jnp.float32)
 
     barrier = pltpu.get_barrier_semaphore()
     greeted = [device(mx, my, z, core) for mx, my in mates_to[1:]]
@@ -200,10 +209,10 @@
 
     @pl.when(across == 1)
     def _():
-        for r in range(CHUNKS):
-            rows = pl.ds(ROUND_ROWS[r] * CHUNK, CHUNK)
+        for r in range(len(ROUNDS)):
+            rows = pl.ds(*ROUNDS[r])
             copy(hidden.at[rows, :], h_ref(own_block, r), send.at[5],
-                 hsem.at[own_block * CHUNKS + r], sibling).start()
+                 h_sem(own_block, r), sibling).start()
 
     def own_weights(i):
         mx, my = mates[i]
@@ -259,12 +268,12 @@
             a = block(left, y_hi, 0)
             h_wait(a, r)
             if r % 2 == 0:
-                h_x(a, r, (1,))
+                pass_on(x_to, 3, 1, a, r)
             h_y(a, r)
             a = block(right, y_hi, 0)
             h_wait(a, r)
             if r % 2 == 1:
-                h_x(a, r, (-1,))
+                pass_on(x_to, 3, -1, a, r)
             h_y(a, r)
 
         @pl.when(across == 1)
@@ -272,12 +281,12 @@
             b = block(x, yh_down, 1)
             h_wait(b, r)
             if r % 2 == 0:
-                h_y(b, r, (1,))
+                pass_on(y_to, 4, 1, b, r)
             h_x(b, r)
             b = block(x, yh_up, 1)
             h_wait(b, r)
             if r % 2 == 1:
-                h_y(b, r, (-1,))
+                pass_on(y_to, 4, -1, b, r)
             h_x(b, r)
 
     def hidden2(r):
@@ -298,22 +307,22 @@
             a = block(xs_steps[m], yh_down, 0)
             h_wait(a, r)
             if (m + r) % 2 == 0:
-                h_y(a, r, (1,))
+                pass_on(y_to, 4, 1, a, r)
             a = block(xs_steps[m], yh_up, 0)
             h_wait(a, r)
             if (m + r) % 2 == 1:
-                h_y(a, r, (-1,))
+                pass_on(y_to, 4, -1, a, r)
 
     def hidden3b(r):
         for yh in range(2):
             b = block(left, yh, 1)
             h_wait(b, r)
             if (yh + r) % 2 == 0:
-                h_x(b, r, (1,))
+                pass_on(x_to, 3, 1, b, r)
             b = block(right, yh, 1)
             h_wait(b, r)
             if (yh + r) % 2 == 1:
-                h_x(b, r, (-1,))
+                pass_on(x_to, 3, -1, b, r)
 
     def hidden4a(m, r):
         @pl.when(across == 0)
@@ -330,17 +339,21 @@
 
         @pl.when(across == 0)
         def _():
-            filters = lax.broadcasted_iota(jnp.int32, (FILTERS, WIDTH), 0)
+            groups = WIDTH // GROUP
+            filters = lax.broadcasted_iota(jnp.int32, (FILTERS, groups), 0)
             selector = (filters == assigned[...]).astype(jnp.float32)
-            taps[...] = jnp.dot(bank8[...], selector, precision=lax.Precision.HIGHEST,
+            picked = jnp.dot(bank8[...], selector, precision=lax.Precision.HIGHEST,
+                             preferred_element_type=jnp.float32)
+            owner = lax.broadcasted_iota(jnp.int32, (groups, WIDTH), 1) // GROUP
+            member = lax.broadcasted_iota(jnp.int32, (groups, WIDTH), 0)
+            taps[...] = jnp.dot(picked, (owner == member).astype(jnp.float32),
+                                precision=lax.Precision.HIGHEST,
                                 preferred_element_type=jnp.float32)
             copy(taps, taps, send.at[6], misc.at[0], sibling).start()
 
         @pl.when(across == 1)
         def _():
             copy(taps, taps, send.at[6], misc.at[0], sibling).wait_recv()
-
-        prod[0:8, :] = jnp.zeros((8, WIDTH), jnp.float32)
 
     codes = [(kind == "x") * 32 + r * 8 + step * 2 + half for kind, r, step, half in DOTS]
     words = [sum(code << 6 * i for i, code in enumerate(codes[first:first + 5]))
@@ -442,8 +455,10 @@
 
     def epilogue3():
         products(2 * CHUNK)
-        filtered(2 * CHUNK, 9, 32)
-        out_send(2 * CHUNK, CHUNK + 32, 8)
+        filtered(2 * CHUNK, 4, 32)
+        out_send(2 * CHUNK, 128, 8)
+        filtered(2 * CHUNK + 128, 5, 32)
+        out_send(2 * CHUNK + 128, 160, 9)
 
     def zero_acc():
         def step(i, _):
@@ -475,7 +490,8 @@
     out_wait(3 * CHUNK + 32, CHUNK - 32, 5)
     out_wait(0, CHUNK, 6)
     out_wait(CHUNK, CHUNK, 7)
-    out_wait(2 * CHUNK, CHUNK + 32, 8)
+    out_wait(2 * CHUNK, 128, 8)
+    out_wait(2 * CHUNK + 128, 160, 9)
 
     def sent(ref, sem):
         copy(ref, ref, send.at[sem], misc.at[0], sibling).wait_send()
@@ -503,7 +519,6 @@
 
 
 def on_device(hidden, in_weights, filter_bank, assignment):
-    assigned = jnp.repeat(assignment, GROUP)[None, :]
     any_space = pl.BlockSpec(memory_space=pl.ANY)
     vmem = pl.BlockSpec(memory_space=pltpu.VMEM)
     return pl.pallas_call(
@@ -520,17 +535,17 @@
             pltpu.VMEM((TOKENS, WIDTH), jnp.bfloat16),
             pltpu.VMEM((8, WIDTH), jnp.float32),
             pltpu.VMEM((8, FILTERS), jnp.float32),
-            pltpu.SemaphoreType.DMA((16 * CHUNKS,)),
+            pltpu.SemaphoreType.DMA((16 * len(ROUNDS),)),
             pltpu.SemaphoreType.DMA((64,)),
             pltpu.SemaphoreType.DMA((8,)),
-            pltpu.SemaphoreType.DMA((9,)),
-            pltpu.SemaphoreType.DMA((9,)),
+            pltpu.SemaphoreType.DMA((10,)),
+            pltpu.SemaphoreType.DMA((10,)),
         ],
         compiler_params=pltpu.CompilerParams(
             collective_id=0, has_side_effects=True, vmem_limit_bytes=60 * 2**20),
         cost_estimate=pl.CostEstimate(
             flops=2 * TOKENS * D * 3 * WIDTH, bytes_accessed=44 * 2**20, transcendentals=0),
-    )(hidden, in_weights, filter_bank, assigned)
+    )(hidden, in_weights, filter_bank, assignment[None, :])
 
 
 def solution(mesh):

time: 164 us -> 162 us (0.988)
  no operation moved by 1% of the time
where the time goes in v4:
time: 162 us; the launch traced here: 160 us
  Pallas kernels  158 us (98%)
  local copies, waits for them, and re-layouts  2.26 us (1%)
    pallas_call x1, Pallas kernels, on_device(): pl.pallas_call(kernel, name='hyena', out_shape=jax.ShapeDtypeStruct((TOKE...  158 us

profile of v4, /device:TPU:1, one launch (start us, length us, event | category | flops | bytes accessed | tf_op | source)
XLA Modules:
  0.0 160.4 jit_solution(1484562998076165927)
XLA Ops:
  0.0 158.1 %hyena.1 = bf16[1024,512]{1,0:T(8,128)(2,1)} custom-call(bf16[1024,512]{1,0:T(8,128)(2,1)} %hidden.1, bf16[64,24576]{1,0:T(8,128)(2,1)} %weights.1, f32[7,512]{1,0:T(8,128)} %bank.1, s32[1,32]{1,0:T(1,128)} %bitcast.1), custom_call_target="tpu_custom_call" | custom-call | flops 25769803776 | bytes 46137344 | tf_op jit(solution)/shard_map/hyena/pallas_call | solution.py:524
  158.2 2.3 %copy.6 = bf16[1024,512]{1,0:T(8,128)(2,1)} copy(bf16[1024,512]{1,0:T(8,128)(2,1)} %hyena.1) | data formatting | bytes 2097152

commit v5 on v4

--- a/solution.py
+++ b/solution.py
@@ -17,9 +17,9 @@
 MESH = pl.DeviceIdType.MESH
 
 ROUNDS = ((768, 256), (0, 256), (256, 256), (512, 256))
-ORDER = ((0, 0), (1, 0), (3, 0), (0, 2), (2, 0), (1, 2), (3, 2), (2, 2),
-         (0, 1), (0, 3), (1, 1), (3, 3), (1, 3), (3, 1), (2, 1), (2, 3))
-STARTS = (19.54, 40.17, 60.8, 81.43)
+ORDER = ((0, 0), (1, 2), (3, 2), (2, 0), (1, 0), (3, 0), (0, 2), (2, 2),
+         (1, 1), (3, 3), (1, 3), (3, 1), (0, 1), (0, 3), (2, 1), (2, 3))
+STARTS = (15.0, 37.0, 60.0, 81.0)
 STAGES = (0.0, 6.54, 23.09, 34.44, 49.63)
 LAST = (12.84, 25.44, 35.22, 44.3, 71.25)
 SPREAD = (2.51, 2.56)

time: 162 us -> 165 us (1.019)
  Pallas kernels: 158 us -> 163 us
    pallas_call x1, Pallas kernels: 158 us -> 163 us  [on_device(): pl.pallas_call(kernel, name='hyena', out_shape=jax.ShapeDtypeStruct((TOKE...]
where the time goes in v5:
time: 165 us
  Pallas kernels  163 us (99%)
  local copies, waits for them, and re-layouts  2.26 us (1%)
    pallas_call x1, Pallas kernels, on_device(): pl.pallas_call(kernel, name='hyena', out_shape=jax.ShapeDtypeStruct((TOKE...  163 us

profile of v5, /device:TPU:1, one launch (start us, length us, event | category | flops | bytes accessed | tf_op | source)
XLA Modules:
  0.0 164.9 jit_solution(12040623861650583327)
XLA Ops:
  0.0 162.6 %hyena.1 = bf16[1024,512]{1,0:T(8,128)(2,1)} custom-call(bf16[1024,512]{1,0:T(8,128)(2,1)} %hidden.1, bf16[64,24576]{1,0:T(8,128)(2,1)} %weights.1, f32[7,512]{1,0:T(8,128)} %bank.1, s32[1,32]{1,0:T(1,128)} %bitcast.1), custom_call_target="tpu_custom_call" | custom-call | flops 25769803776 | bytes 46137344 | tf_op jit(solution)/shard_map/hyena/pallas_call | solution.py:524
  162.6 2.3 %copy.6 = bf16[1024,512]{1,0:T(8,128)(2,1)} copy(bf16[1024,512]{1,0:T(8,128)(2,1)} %hyena.1) | data formatting | bytes 2097152

commit v6 on v4

--- a/solution.py
+++ b/solution.py
@@ -19,7 +19,7 @@
 ROUNDS = ((768, 256), (0, 256), (256, 256), (512, 256))
 ORDER = ((0, 0), (1, 0), (3, 0), (0, 2), (2, 0), (1, 2), (3, 2), (2, 2),
          (0, 1), (0, 3), (1, 1), (3, 3), (1, 3), (3, 1), (2, 1), (2, 3))
-STARTS = (19.54, 40.17, 60.8, 81.43)
+STARTS = (15.0, 37.0, 60.0, 81.0)
 STAGES = (0.0, 6.54, 23.09, 34.44, 49.63)
 LAST = (12.84, 25.44, 35.22, 44.3, 71.25)
 SPREAD = (2.51, 2.56)

time: 162 us -> 165 us (1.019)
  Pallas kernels: 158 us -> 162 us
    pallas_call x1, Pallas kernels: 158 us -> 162 us  [on_device(): pl.pallas_call(kernel, name='hyena', out_shape=jax.ShapeDtypeStruct((TOKE...]
where the time goes in v6:
time: 165 us; the launch traced here: 164 us
  Pallas kernels  162 us (98%)
  local copies, waits for them, and re-layouts  2.26 us (1%)
    pallas_call x1, Pallas kernels, on_device(): pl.pallas_call(kernel, name='hyena', out_shape=jax.ShapeDtypeStruct((TOKE...  162 us

profile of v6, /device:TPU:1, one launch (start us, length us, event | category | flops | bytes accessed | tf_op | source)
XLA Modules:
  0.0 164.5 jit_solution(8964672714446742946)
XLA Ops:
  0.0 162.2 %hyena.1 = bf16[1024,512]{1,0:T(8,128)(2,1)} custom-call(bf16[1024,512]{1,0:T(8,128)(2,1)} %hidden.1, bf16[64,24576]{1,0:T(8,128)(2,1)} %weights.1, f32[7,512]{1,0:T(8,128)} %bank.1, s32[1,32]{1,0:T(1,128)} %bitcast.1), custom_call_target="tpu_custom_call" | custom-call | flops 25769803776 | bytes 46137344 | tf_op jit(solution)/shard_map/hyena/pallas_call | solution.py:524
  162.2 2.3 %copy.6 = bf16[1024,512]{1,0:T(8,128)(2,1)} copy(bf16[1024,512]{1,0:T(8,128)(2,1)} %hyena.1) | data formatting | bytes 2097152

commit v7 on v4

--- a/solution.py
+++ b/solution.py
@@ -50,7 +50,7 @@
 
 
 def timeline():
-    when = {("taps",): 30.0, ("zero",): 33.0}
+    when = {("taps",): 30.0}
     for i in range(16):
         if i:
             when["all", i] = ALL[0] + ALL[1] * i
@@ -192,12 +192,38 @@
 
     prod[0:8, :] = jnp.zeros((8, WIDTH), jnp.float32)
 
+    def pick_taps():
+        bank8[0:TAPS, :] = bank[...]
+        bank8[TAPS:, :] = jnp.zeros((8 - TAPS, FILTERS), jnp.float32)
+
+        @pl.when(across == 0)
+        def _():
+            groups = WIDTH // GROUP
+            filters = lax.broadcasted_iota(jnp.int32, (FILTERS, groups), 0)
+            selector = (filters == assigned[...]).astype(jnp.float32)
+            picked = jnp.dot(bank8[...], selector, precision=lax.Precision.HIGHEST,
+                             preferred_element_type=jnp.float32)
+            owner = lax.broadcasted_iota(jnp.int32, (groups, WIDTH), 1) // GROUP
+            member = lax.broadcasted_iota(jnp.int32, (groups, WIDTH), 0)
+            taps[...] = jnp.dot(picked, (owner == member).astype(jnp.float32),
+                                precision=lax.Precision.HIGHEST,
+                                preferred_element_type=jnp.float32)
+
+    def zero_acc():
+        def step(i, _):
+            rows = pl.ds(pl.multiple_of(i * 32, 32), 32)
+            acc[rows, :] = jnp.zeros((32, 3 * WIDTH), jnp.float32)
+            return 0
+        lax.fori_loop(0, TOKENS // 32, step, 0)
+
     barrier = pltpu.get_barrier_semaphore()
     greeted = [device(mx, my, z, core) for mx, my in mates_to[1:]]
     greeted += [z_to[1], z_to[-1], sibling, partner,
                 device(x, y, above, 1 - core), device(x, y, below, 1 - core)]
     for to in greeted:
         pl.semaphore_signal(barrier, inc=1, device_id=to, device_id_type=MESH)
+    zero_acc()
+    pick_taps()
     pl.semaphore_wait(barrier, len(greeted))
 
     def all_to_all(i):
@@ -333,22 +359,9 @@
         for yh in range(2):
             h_wait(block((x + 2) % 4, yh, 1), r)
 
-    def make_taps():
-        bank8[0:TAPS, :] = bank[...]
-        bank8[TAPS:, :] = jnp.zeros((8 - TAPS, FILTERS), jnp.float32)
-
-        @pl.when(across == 0)
-        def _():
-            groups = WIDTH // GROUP
-            filters = lax.broadcasted_iota(jnp.int32, (FILTERS, groups), 0)
-            selector = (filters == assigned[...]).astype(jnp.float32)
-            picked = jnp.dot(bank8[...], selector, precision=lax.Precision.HIGHEST,
-                             preferred_element_type=jnp.float32)
-            owner = lax.broadcasted_iota(jnp.int32, (groups, WIDTH), 1) // GROUP
-            member = lax.broadcasted_iota(jnp.int32, (groups, WIDTH), 0)
-            taps[...] = jnp.dot(picked, (owner == member).astype(jnp.float32),
-                                precision=lax.Precision.HIGHEST,
-                                preferred_element_type=jnp.float32)
+    def share_taps():
+        @pl.when(across == 0)
+        def _():
             copy(taps, taps, send.at[6], misc.at[0], sibling).start()
 
         @pl.when(across == 1)
@@ -460,14 +473,7 @@
         filtered(2 * CHUNK + 128, 5, 32)
         out_send(2 * CHUNK + 128, 160, 9)
 
-    def zero_acc():
-        def step(i, _):
-            rows = pl.ds(pl.multiple_of(i * 32, 32), 32)
-            acc[rows, :] = jnp.zeros((32, 3 * WIDTH), jnp.float32)
-            return 0
-        lax.fori_loop(0, TOKENS // 32, step, 0)
-
-    run = {"taps": make_taps, "zero": zero_acc, "all": all_to_all, "own": own_weights, "near": near_weights, "far": far_weights, "sib": sib_wait,
+    run = {"taps": share_taps, "all": all_to_all, "own": own_weights, "near": near_weights, "far": far_weights, "sib": sib_wait,
            "h0": hidden0, "h0b": hidden0b, "h1": hidden1, "h2": hidden2, "h3a": hidden3a, "h3b": hidden3b,
            "h4a": hidden4a, "h4b": hidden4b}
     before = timeline()

time: 162 us -> 162 us (level)
  no operation moved by 1% of the time
where the time goes in v7:
time: 162 us; the launch traced here: 160 us
  Pallas kernels  158 us (98%)
  local copies, waits for them, and re-layouts  2.26 us (1%)
    pallas_call x1, Pallas kernels, on_device(): pl.pallas_call(kernel, name='hyena', out_shape=jax.ShapeDtypeStruct((TOKE...  158 us

profile of v7, /device:TPU:1, one launch (start us, length us, event | category | flops | bytes accessed | tf_op | source)
XLA Modules:
  0.0 160.4 jit_solution(10162366094640778265)
XLA Ops:
  0.0 158.1 %hyena.1 = bf16[1024,512]{1,0:T(8,128)(2,1)} custom-call(bf16[1024,512]{1,0:T(8,128)(2,1)} %hidden.1, bf16[64,24576]{1,0:T(8,128)(2,1)} %weights.1, f32[7,512]{1,0:T(8,128)} %bank.1, s32[1,32]{1,0:T(1,128)} %bitcast.1), custom_call_target="tpu_custom_call" | custom-call | flops 25769803776 | bytes 46137344 | tf_op jit(solution)/shard_map/hyena/pallas_call | solution.py:530
  158.2 2.3 %copy.6 = bf16[1024,512]{1,0:T(8,128)(2,1)} copy(bf16[1024,512]{1,0:T(8,128)(2,1)} %hyena.1) | data formatting | bytes 2097152
